TPU v7x, 32 devices: a whole 2x2x4 slice. The times are simulated.
32 devices in a mesh: dp: 8 (over z, x), fsdp: 4 (over y, core).
Axes of the slice: x: 2, y: 2, z: 4, core: 2. Of those that a mesh axis runs over, the one named last changes fastest.
Arguments:
- tokens: bfloat16 [73728, 640], P(('dp', 'fsdp')), may hold values from -6 to 6
- cotangent: bfloat16 [73728, 640], P(('dp', 'fsdp')), may hold values from -6 to 6
- lengths: int32 [64, 4], P(('dp', 'fsdp')), may hold values from 1 to 1024, 1152 in all within a row
- w_query: bfloat16 [640, 1024], P(None, ('dp', 'fsdp')), may hold values from -0.25 to 0.25
- w_key: bfloat16 [640, 256], P(None, ('dp', 'fsdp')), may hold values from -0.25 to 0.25
- w_value: bfloat16 [640, 256], P(None, ('dp', 'fsdp')), may hold values from -0.25 to 0.25
- w_out: bfloat16 [1024, 640], P(('dp', 'fsdp')), may hold values from -0.1875 to 0.1875
- w_gate: bfloat16 [640, 2048], P(None, ('dp', 'fsdp')), may hold values from -0.25 to 0.25
- w_up: bfloat16 [640, 2048], P(None, ('dp', 'fsdp')), may hold values from -0.25 to 0.25
- w_down: bfloat16 [2048, 640], P(('dp', 'fsdp')), may hold values from -0.125 to 0.125
- gain_pre_attn: float32 [640], replicated, may hold values from 0.25 to 1.75
- gain_query: float32 [256], replicated, may hold values from 0.25 to 1.75
- gain_key: float32 [256], replicated, may hold values from 0.25 to 1.75
- gain_post_attn: float32 [640], replicated, may hold values from 0.25 to 1.75
- gain_pre_ff: float32 [640], replicated, may hold values from 0.25 to 1.75
- gain_post_ff: float32 [640], replicated, may hold values from 0.25 to 1.75
Outputs:
- layer_out: bfloat16 [73728, 640], P(('dp', 'fsdp'))
- grad_tokens: float32 [73728, 640], P(('dp', 'fsdp'))
- grad_query: float32 [640, 1024], P(None, ('dp', 'fsdp'))
- grad_key: float32 [640, 256], P(None, ('dp', 'fsdp'))
- grad_value: float32 [640, 256], P(None, ('dp', 'fsdp'))
- grad_out: float32 [1024, 640], P(('dp', 'fsdp'))
- grad_gate: float32 [640, 2048], P(None, ('dp', 'fsdp'))
- grad_up: float32 [640, 2048], P(None, ('dp', 'fsdp'))
- grad_down: float32 [2048, 640], P(('dp', 'fsdp'))
- grad_pre_attn: float32 [640], replicated
- grad_gain_query: float32 [256], replicated
- grad_gain_key: float32 [256], replicated
- grad_post_attn: float32 [640], replicated
- grad_pre_ff: float32 [640], replicated
- grad_post_ff: float32 [640], replicated
Inputs may be any that keep to these rules, and one draw needn't show every extreme that they name: Each micro-batch's 4 lengths sum to 1152, and its longest document has exactly 1024 tokens.
All inputs are finite; a program needn't handle non-finite values.
Results may differ from a plain program's by a relative error of at most 0.017.
Values may be sent and summed in bfloat16 or wider, within the bound.
No kernel may reach another device: no remote copies, remote signals or barrier semaphores. Data moves between devices by JAX's collectives and lax.ppermute only.
A program may use at most 256 MiB of HBM per device.

v0:
```python
import math

import jax
import jax.numpy as jnp
from jax import lax
from jax.sharding import PartitionSpec as P

HQ = 4
HD = 256
WINDOW = 512


epsilon = 1e-06


def rms_scale(values, scale_gain):
    return (
        values * lax.rsqrt(jnp.mean(values * values, axis=-1, keepdims=True) + epsilon) * scale_gain
    )


def rotate(values, angles):
    half_size = values.shape[-1] // 2
    cos_part = jnp.cos(angles)[:, None, :]
    sin_part = jnp.sin(angles)[:, None, :]
    leading = values[..., :half_size]
    trailing = values[..., half_size:]
    return jnp.concatenate(
        [leading * cos_part - trailing * sin_part, trailing * cos_part + leading * sin_part],
        axis=-1,
    )


def layout(doc_lengths, row_count, window_size, head_size):
    places = jnp.arange(row_count, dtype=jnp.int32)
    doc_ends = jnp.cumsum(doc_lengths)
    passed = places[:, None] >= doc_ends[None, :]
    doc_index = jnp.sum(passed.astype(jnp.int32), axis=1)
    doc_start = jnp.sum(jnp.where(passed, doc_lengths[None, :], 0), axis=1)
    position = (places - doc_start).astype(jnp.float32)
    steps_back = places[:, None] - places[None, :]
    visible = (
        (doc_index[:, None] == doc_index[None, :]) & (steps_back >= 0) & (steps_back < window_size)
    )
    frequency = jnp.exp(
        jnp.arange(head_size // 2, dtype=jnp.float32) * (-2.0 * math.log(10000.0) / head_size)
    )
    angles = position[:, None] * frequency[None, :]
    return (angles, visible)


def head_prep(query_raw, key_raw, gain_query, gain_key, angles):
    row_count = query_raw.shape[0]
    queries = rotate(rms_scale(query_raw.reshape(row_count, HQ, HD), gain_query), angles)
    keys_rot = rotate(rms_scale(key_raw[:, None, :], gain_key), angles)[:, 0, :]
    return (queries, keys_rot)


def gelu_product(gate_pre, up_pre):
    return jax.nn.gelu(gate_pre, approximate=True) * up_pre


def product(form, left, right):
    return jnp.einsum(form, left, right, preferred_element_type=jnp.float32)


def body(
    tokens,
    cotangent,
    lengths,
    w_query,
    w_key,
    w_value,
    w_out,
    w_gate,
    w_up,
    w_down,
    gain_pre_attn,
    gain_query,
    gain_key,
    gain_post_attn,
    gain_pre_ff,
    gain_post_ff,
):
    micro_count = lengths.shape[0]
    row_count = tokens.shape[0] // micro_count
    feature_width = tokens.shape[1]
    sources = tokens.reshape(micro_count, row_count, feature_width)
    cot_rows = cotangent.reshape(micro_count, row_count, feature_width)
    scale_factor = HD ** (-0.5)
    devices_all = lax.axis_size(("dp", "fsdp"))

    def micro_step(running, inputs_mb):
        source, cot_row, doc_lengths = inputs_mb
        angles, visible = layout(doc_lengths, row_count, WINDOW, HD)
        forward_w = (
            lax.all_gather(w_query, ("dp", "fsdp"), axis=1, tiled=True),
            lax.all_gather(w_key, ("dp", "fsdp"), axis=1, tiled=True),
            lax.all_gather(w_value, ("dp", "fsdp"), axis=1, tiled=True),
            lax.all_gather(w_out, ("dp", "fsdp"), axis=0, tiled=True),
            lax.all_gather(w_gate, ("dp", "fsdp"), axis=1, tiled=True),
            lax.all_gather(w_up, ("dp", "fsdp"), axis=1, tiled=True),
            lax.all_gather(w_down, ("dp", "fsdp"), axis=0, tiled=True),
        )
        full_query, full_key, full_value, full_out, full_gate, full_up, full_down = forward_w
        source_f = source.astype(jnp.float32)
        normed, back_pre_attn = jax.vjp(rms_scale, source_f, gain_pre_attn)
        normed_b = normed.astype(jnp.bfloat16)
        query_raw = jnp.dot(normed_b, full_query, preferred_element_type=jnp.float32)
        key_raw = jnp.dot(normed_b, full_key, preferred_element_type=jnp.float32)
        value_b = jnp.dot(normed_b, full_value, preferred_element_type=jnp.float32).astype(
            jnp.bfloat16
        )
        (queries, keys_rot), back_heads = jax.vjp(
            lambda q, k, a, b: head_prep(q, k, a, b, angles),
            query_raw,
            key_raw,
            gain_query,
            gain_key,
        )
        queries_b = queries.astype(jnp.bfloat16)
        keys_b = keys_rot.astype(jnp.bfloat16)
        scores = product("rhd,cd->hrc", queries_b, keys_b) * scale_factor
        scores = jnp.where(visible[None], scores, -1e30)
        row_max = jnp.max(scores, axis=-1, keepdims=True)
        exponent = jnp.exp(scores - row_max)
        row_sum = jnp.sum(exponent, axis=-1, keepdims=True)
        attention_b = (exponent / row_sum).astype(jnp.bfloat16)
        log_total = row_max + jnp.log(row_sum)
        context_b = (
            product("hrc,cd->rhd", attention_b, value_b)
            .astype(jnp.bfloat16)
            .reshape(row_count, HQ * HD)
        )
        branch = jnp.dot(context_b, full_out, preferred_element_type=jnp.float32)
        branch_normed, back_post_attn = jax.vjp(rms_scale, branch, gain_post_attn)
        middle = source_f + branch_normed
        normed_ff, back_pre_ff = jax.vjp(rms_scale, middle, gain_pre_ff)
        normed_ff_b = normed_ff.astype(jnp.bfloat16)
        gate_pre = jnp.dot(normed_ff_b, full_gate, preferred_element_type=jnp.float32)
        up_pre = jnp.dot(normed_ff_b, full_up, preferred_element_type=jnp.float32)
        hidden, back_gelu = jax.vjp(gelu_product, gate_pre, up_pre)
        hidden_b = hidden.astype(jnp.bfloat16)
        down_out = jnp.dot(hidden_b, full_down, preferred_element_type=jnp.float32)
        down_normed, back_post_ff = jax.vjp(rms_scale, down_out, gain_post_ff)
        result = (middle + down_normed).astype(jnp.bfloat16)
        backward_w = (
            lax.all_gather(w_query, ("dp", "fsdp"), axis=1, tiled=True),
            lax.all_gather(w_key, ("dp", "fsdp"), axis=1, tiled=True),
            lax.all_gather(w_value, ("dp", "fsdp"), axis=1, tiled=True),
            lax.all_gather(w_out, ("dp", "fsdp"), axis=0, tiled=True),
            lax.all_gather(w_gate, ("dp", "fsdp"), axis=1, tiled=True),
            lax.all_gather(w_up, ("dp", "fsdp"), axis=1, tiled=True),
            lax.all_gather(w_down, ("dp", "fsdp"), axis=0, tiled=True),
        )
        back_query, back_key, back_value, back_out, back_gate, back_up, back_down = backward_w
        upstream = cot_row.astype(jnp.float32)
        d_down, d_gain_post_ff = back_post_ff(upstream)
        d_down_b = d_down.astype(jnp.bfloat16)
        grad_down_mb = product("rf,rd->fd", hidden_b, d_down_b)
        d_hidden = product("rd,fd->rf", d_down_b, back_down)
        d_gate, d_up = back_gelu(d_hidden)
        d_gate_b = d_gate.astype(jnp.bfloat16)
        d_up_b = d_up.astype(jnp.bfloat16)
        grad_gate_mb = product("rd,rf->df", normed_ff_b, d_gate_b)
        grad_up_mb = product("rd,rf->df", normed_ff_b, d_up_b)
        d_normed_ff = product("rf,df->rd", d_gate_b, back_gate) + product(
            "rf,df->rd", d_up_b, back_up
        )
        d_middle_part, d_gain_pre_ff = back_pre_ff(d_normed_ff)
        d_middle = upstream + d_middle_part
        d_branch, d_gain_post_attn = back_post_attn(d_middle)
        d_branch_b = d_branch.astype(jnp.bfloat16)
        grad_out_mb = product("rk,rd->kd", context_b, d_branch_b)
        d_context_b = (
            product("rd,kd->rk", d_branch_b, back_out)
            .astype(jnp.bfloat16)
            .reshape(row_count, HQ, HD)
        )
        scores_again = product("rhd,cd->hrc", queries_b, keys_b) * scale_factor
        scores_again = jnp.where(visible[None], scores_again, -1e30)
        attention_f = jnp.exp(scores_again - log_total)
        d_attention = product("rhd,cd->hrc", d_context_b, value_b)
        row_dot = jnp.sum(attention_f * d_attention, axis=-1, keepdims=True)
        d_scores_b = (attention_f * (d_attention - row_dot)).astype(jnp.bfloat16)
        d_queries = product("hrc,cd->rhd", d_scores_b, keys_b) * scale_factor
        d_keys = product("hrc,rhd->cd", d_scores_b, queries_b) * scale_factor
        d_value_b = product("hrc,rhd->cd", attention_b, d_context_b).astype(jnp.bfloat16)
        d_query_raw, d_key_raw, d_gain_query, d_gain_key = back_heads((d_queries, d_keys))
        d_query_b = d_query_raw.astype(jnp.bfloat16)
        d_key_b = d_key_raw.astype(jnp.bfloat16)
        grad_query_mb = product("rd,rk->dk", normed_b, d_query_b)
        grad_key_mb = product("rd,rk->dk", normed_b, d_key_b)
        grad_value_mb = product("rd,rk->dk", normed_b, d_value_b)
        d_normed = (
            product("rk,dk->rd", d_query_b, back_query)
            + product("rk,dk->rd", d_key_b, back_key)
            + product("rk,dk->rd", d_value_b, back_value)
        )
        d_source_part, d_gain_pre_attn = back_pre_attn(d_normed)
        grad_source = d_middle + d_source_part
        terms = (
            grad_query_mb,
            grad_key_mb,
            grad_value_mb,
            grad_out_mb,
            grad_gate_mb,
            grad_up_mb,
            grad_down_mb,
            d_gain_pre_attn,
            d_gain_query,
            d_gain_key,
            d_gain_post_attn,
            d_gain_pre_ff,
            d_gain_post_ff,
        )
        running = tuple((total_part + term_part for total_part, term_part in zip(running, terms)))
        return (running, (result, grad_source))

    zeros_init = (
        jnp.zeros((feature_width, w_query.shape[1] * devices_all), jnp.float32),
        jnp.zeros((feature_width, w_key.shape[1] * devices_all), jnp.float32),
        jnp.zeros((feature_width, w_value.shape[1] * devices_all), jnp.float32),
        jnp.zeros((w_out.shape[0] * devices_all, feature_width), jnp.float32),
        jnp.zeros((feature_width, w_gate.shape[1] * devices_all), jnp.float32),
        jnp.zeros((feature_width, w_up.shape[1] * devices_all), jnp.float32),
        jnp.zeros((w_down.shape[0] * devices_all, feature_width), jnp.float32),
        jnp.zeros_like(gain_pre_attn),
        jnp.zeros_like(gain_query),
        jnp.zeros_like(gain_key),
        jnp.zeros_like(gain_post_attn),
        jnp.zeros_like(gain_pre_ff),
        jnp.zeros_like(gain_post_ff),
    )
    sums, outputs = lax.scan(micro_step, zeros_init, (sources, cot_rows, lengths))
    results, grad_sources = outputs
    weight_parts = (
        lax.psum_scatter(sums[0], ("dp", "fsdp"), scatter_dimension=1, tiled=True),
        lax.psum_scatter(sums[1], ("dp", "fsdp"), scatter_dimension=1, tiled=True),
        lax.psum_scatter(sums[2], ("dp", "fsdp"), scatter_dimension=1, tiled=True),
        lax.psum_scatter(sums[3], ("dp", "fsdp"), scatter_dimension=0, tiled=True),
        lax.psum_scatter(sums[4], ("dp", "fsdp"), scatter_dimension=1, tiled=True),
        lax.psum_scatter(sums[5], ("dp", "fsdp"), scatter_dimension=1, tiled=True),
        lax.psum_scatter(sums[6], ("dp", "fsdp"), scatter_dimension=0, tiled=True),
    )
    gain_parts = lax.psum((sums[7], sums[8], sums[9], sums[10], sums[11], sums[12]), ("dp", "fsdp"))
    return (
        results.reshape(micro_count * row_count, feature_width),
        grad_sources.reshape(micro_count * row_count, feature_width),
        weight_parts[0],
        weight_parts[1],
        weight_parts[2],
        weight_parts[3],
        weight_parts[4],
        weight_parts[5],
        weight_parts[6],
        gain_parts[0],
        gain_parts[1],
        gain_parts[2],
        gain_parts[3],
        gain_parts[4],
        gain_parts[5],
    )


def solution(mesh):
    placed = (
        P(("dp", "fsdp"), None),
        P(("dp", "fsdp"), None),
        P(("dp", "fsdp"), None),
        P(None, ("dp", "fsdp")),
        P(None, ("dp", "fsdp")),
        P(None, ("dp", "fsdp")),
        P(("dp", "fsdp"), None),
        P(None, ("dp", "fsdp")),
        P(None, ("dp", "fsdp")),
        P(("dp", "fsdp"), None),
        P(),
        P(),
        P(),
        P(),
        P(),
        P(),
    )
    return jax.shard_map(
        body,
        mesh=mesh,
        in_specs=placed,
        out_specs=(
            P(("dp", "fsdp"), None),
            P(("dp", "fsdp"), None),
            P(None, ("dp", "fsdp")),
            P(None, ("dp", "fsdp")),
            P(None, ("dp", "fsdp")),
            P(("dp", "fsdp"), None),
            P(None, ("dp", "fsdp")),
            P(None, ("dp", "fsdp")),
            P(("dp", "fsdp"), None),
            P(),
            P(),
            P(),
            P(),
            P(),
            P(),
        ),
        check_vma=False,
    )
```

profile of v0, /device:TPU:0, one launch (start us, length us, event | category | flops | bytes accessed | tf_op | source)
XLA Modules:
  0.0 1743.5 jit_solution(15421538219609553896)
XLA Ops:
  8.2 890.2 %while.41 = (s32[]{:T(128)}, f32[640,1024]{1,0:T(8,128)}, f32[640,256]{1,0:T(8,128)}, f32[640,256]{1,0:T(8,128)}, f32[1024,640]{1,0:T(8,128)}, /*index=5*/f32[64...) while((s32[]{:T(128)}, f32[640,1024]{1,0:T(8,128)}, ...), condition=%wide.region_25.26_spmd.clone, body=%wide.region_0.25_spmd.clone.sunk | while | flops 55117451264 | bytes 1202328448 | solution.py:235
  12.8 44.8 %all_gather.65 = bf16[640,256]{0,1:T(8,128)(2,1)S(1)} all-gather(bf16[640,8]{0,1:T(8,128)(2,1)} %get-tuple-element.1148), channel_id=1, replica_groups=mesh['dp'=8,'fsdp'=4] {'dp','fsdp'}, dimensions={1}, use_global_device_ids=true | all-gather | bytes 337920 | tf_op jit(solution)/shard_map/while/body/eval_jaxpr/all_gather | solution.py:99
  57.6 40.5 %all_gather.64 = bf16[640,256]{0,1:T(8,128)(2,1)} all-gather(bf16[640,8]{0,1:T(8,128)(2,1)} %get-tuple-element.1143), channel_id=1, replica_groups=mesh['dp'=8,'fsdp'=4] {'dp','fsdp'}, dimensions={1}, use_global_device_ids=true | all-gather | bytes 337920 | tf_op jit(solution)/shard_map/while/body/eval_jaxpr/all_gather | solution.py:98
  122.4 10.0 fusion.267
  132.4 9.2 fusion.268
  163.9 21.5 %all-gather.10.cloned.1.call-done = bf16[640,2048]{0,1:T(8,128)(2,1)} async-done(((bf16[640,64]{0,1:T(8,128)(2,1)}), bf16[640,2048]{0,1:T(8,128)(2,1)}) %all-gather.10.cloned.1.call-update) | async-done | bytes 2621456 | tf_op jit(solution)/shard_map/while/body/eval_jaxpr/all_gather | solution.py:101
  185.5 9.6 fusion.272
  195.1 50.0 %all-gather.12.cloned.1.call-done = bf16[640,2048]{0,1:T(8,128)(2,1)} async-done(((bf16[640,64]{0,1:T(8,128)(2,1)}), bf16[640,2048]{0,1:T(8,128)(2,1)}) %all-gather.12.cloned.1.call-update) | async-done | bytes 2621456 | tf_op jit(solution)/shard_map/while/body/eval_jaxpr/all_gather | solution.py:102
  245.1 12.2 multiply_convert_fusion.9
  257.4 47.4 %all-gather.14.cloned.1.call-done = bf16[2048,640]{1,0:T(8,128)(2,1)} async-done(((bf16[64,640]{1,0:T(8,128)(2,1)}), bf16[2048,640]{1,0:T(8,128)(2,1)}) %all-gather.14.cloned.1.call-update) | async-done | bytes 2621456 | tf_op jit(solution)/shard_map/while/body/eval_jaxpr/all_gather | solution.py:103
  304.8 7.2 multiply_reduce_fusion.25
  316.6 15.8 multiply_convert_fusion.10
  332.4 6.2 fusion.276
  338.7 6.9 multiply_reduce_fusion.26
  356.2 13.3 multiply_reduce_fusion.28
  369.5 14.8 multiply_convert_fusion.11
  388.6 5.0 fusion.278
  393.7 9.0 select_add_fusion.23
  407.2 4.6 select_add_fusion.22
  411.9 4.5 select_add_fusion.21
  457.3 40.7 %all_gather.65 = bf16[640,256]{0,1:T(8,128)(2,1)S(1)} all-gather(bf16[640,8]{0,1:T(8,128)(2,1)} %get-tuple-element.1148), channel_id=1, replica_groups=mesh['dp'=8,'fsdp'=4] {'dp','fsdp'}, dimensions={1}, use_global_device_ids=true | all-gather | bytes 337920 | tf_op jit(solution)/shard_map/while/body/eval_jaxpr/all_gather | solution.py:99
  498.0 40.5 %all_gather.64 = bf16[640,256]{0,1:T(8,128)(2,1)} all-gather(bf16[640,8]{0,1:T(8,128)(2,1)} %get-tuple-element.1143), channel_id=1, replica_groups=mesh['dp'=8,'fsdp'=4] {'dp','fsdp'}, dimensions={1}, use_global_device_ids=true | all-gather | bytes 337920 | tf_op jit(solution)/shard_map/while/body/eval_jaxpr/all_gather | solution.py:98
  562.7 9.6 fusion.267
  572.4 9.2 fusion.268
  603.9 21.8 %all-gather.10.cloned.1.call-done = bf16[640,2048]{0,1:T(8,128)(2,1)} async-done(((bf16[640,64]{0,1:T(8,128)(2,1)}), bf16[640,2048]{0,1:T(8,128)(2,1)}) %all-gather.10.cloned.1.call-update) | async-done | bytes 2621456 | tf_op jit(solution)/shard_map/while/body/eval_jaxpr/all_gather | solution.py:101
  625.7 9.6 fusion.272
  635.4 50.2 %all-gather.12.cloned.1.call-done = bf16[640,2048]{0,1:T(8,128)(2,1)} async-done(((bf16[640,64]{0,1:T(8,128)(2,1)}), bf16[640,2048]{0,1:T(8,128)(2,1)}) %all-gather.12.cloned.1.call-update) | async-done | bytes 2621456 | tf_op jit(solution)/shard_map/while/body/eval_jaxpr/all_gather | solution.py:102
  685.5 12.5 multiply_convert_fusion.9
  698.0 47.2 %all-gather.14.cloned.1.call-done = bf16[2048,640]{1,0:T(8,128)(2,1)} async-done(((bf16[64,640]{1,0:T(8,128)(2,1)}), bf16[2048,640]{1,0:T(8,128)(2,1)}) %all-gather.14.cloned.1.call-update) | async-done | bytes 2621456 | tf_op jit(solution)/shard_map/while/body/eval_jaxpr/all_gather | solution.py:103
  745.2 7.2 multiply_reduce_fusion.25
  757.0 15.7 multiply_convert_fusion.10
  772.8 6.2 fusion.276
  779.0 6.9 multiply_reduce_fusion.26
  796.4 13.2 multiply_reduce_fusion.28
  809.7 14.8 multiply_convert_fusion.11
  828.8 5.3 fusion.278
  834.1 10.6 select_add_fusion.23
  849.1 4.6 select_add_fusion.22
  853.8 4.5 select_add_fusion.21
  906.6 5.9 copy.123
  912.6 5.9 copy.124
  919.3 38.9 %all-reduce.6 = (f32[640]{0:T(1024)}, f32[256]{0:T(256)}, f32[256]{0:T(256)}, f32[640]{0:T(1024)}, f32[640]{0:T(1024)}, /*index=5*/f32[640]{0:T(1024)}) all-reduce(f32[640]{0:T(1024)S(1)} %copy-done.80, f32[256]{0:T(256)S(1)} %copy-done.88, f32[256]{0:T(256)S(1)} %copy-done.85, ...), channel_id=1, replica_groups=mesh['dp'=8,'fsdp'=4] {'dp','fsdp'}, use_global_device_ids=true, to_apply=%region_33.34 | all-reduce | flops 3072 | bytes 24576 | tf_op jit(solution)/shard_map/psum | solution.py:246
  958.1 76.7 %all-reduce.10.cloned.1.call-done = (f32[640,256]{0,1:T(8,128)}, f32[640,256]{0,1:T(8,128)}) async-done(((f32[640,256]{0,1:T(8,128)}, f32[640,256]{0,1:T(8,128)}), (f32[640,256]{0,1:T(8,128)}, f32[640,256]{0,1:T(8,128)})) %all-reduce.10.cloned.1.call-update) | async-done | bytes 1310736
  1036.2 137.6 %reduce-scatter.8.cloned.1.call-done = f32[32,640]{1,0:T(8,128)} async-done(((f32[1024,640]{1,0:T(8,128)}), f32[32,640]{1,0:T(8,128)}) %reduce-scatter.8.cloned.1.call-update) | async-done | bytes 81936 | tf_op jit(solution)/shard_map/reduce_scatter | solution.py:241
  1173.8 136.1 %reduce-scatter.6.cloned.1.call-done = f32[640,32]{0,1:T(8,128)} async-done(((f32[640,1024]{0,1:T(8,128)}), f32[640,32]{0,1:T(8,128)}) %reduce-scatter.6.cloned.1.call-update) | async-done | bytes 81936 | tf_op jit(solution)/shard_map/reduce_scatter | solution.py:238
  1309.8 142.0 %reduce-scatter.14.cloned.1.call-done = f32[64,640]{1,0:T(8,128)} async-done(((f32[2048,640]{1,0:T(8,128)}), f32[64,640]{1,0:T(8,128)}) %reduce-scatter.14.cloned.1.call-update) | async-done | bytes 163856 | tf_op jit(solution)/shard_map/reduce_scatter | solution.py:244
  1451.9 142.0 %reduce-scatter.10.cloned.1.call-done = f32[640,64]{0,1:T(8,128)} async-done(((f32[640,2048]{0,1:T(8,128)}), f32[640,64]{0,1:T(8,128)}) %reduce-scatter.10.cloned.1.call-update) | async-done | bytes 163856 | tf_op jit(solution)/shard_map/reduce_scatter | solution.py:242
  1593.8 142.0 %reduce-scatter.12.cloned.1.call-done = f32[640,64]{0,1:T(8,128)} async-done(((f32[640,2048]{0,1:T(8,128)}), f32[640,64]{0,1:T(8,128)}) %reduce-scatter.12.cloned.1.call-update) | async-done | bytes 163856 | tf_op jit(solution)/shard_map/reduce_scatter | solution.py:243
  (619 shorter events, 231.1 us)
Async XLA Ops:
  8.4 106.6 %all-gather.6.cloned.1.call-start = ((), (), s32[]{:S(2)}) async-start(), calls=%async_computation.11 | async-start | bytes 1351680 | tf_op jit(solution)/shard_map/while/body/eval_jaxpr/all_gather | solution.py:97
  9.2 147.4 %all-gather.8.cloned.1.call-start = ((), (), s32[]{:S(2)}) async-start(), calls=%async_computation.12 | async-start | bytes 1351680 | tf_op jit(solution)/shard_map/while/body/eval_jaxpr/all_gather | solution.py:100
  9.9 175.5 %all-gather.10.cloned.1.call-start = ((), (), s32[]{:S(2)}) async-start(), calls=%async_computation.13 | async-start | bytes 2703360 | tf_op jit(solution)/shard_map/while/body/eval_jaxpr/all_gather | solution.py:101
  10.7 234.5 %all-gather.12.cloned.1.call-start = ((), (), s32[]{:S(2)}) async-start(), calls=%async_computation.14 | async-start | bytes 2703360 | tf_op jit(solution)/shard_map/while/body/eval_jaxpr/all_gather | solution.py:102
  11.2 293.6 %all-gather.14.cloned.1.call-start = ((), (), s32[]{:S(2)}) async-start(), calls=%async_computation.15 | async-start | bytes 2703360 | tf_op jit(solution)/shard_map/while/body/eval_jaxpr/all_gather | solution.py:103
  11.8 100.5 %copy-start.81 = (f32[128]{0:T(128)}, f32[128]{0:T(128)S(1)}, u32[]{:S(2)}) copy-start(f32[128]{0:T(128)S(1)} %multiply_exponential_fusion.2) | copy-start | bytes 1540 | tf_op jit(solution)/shard_map/while
  12.8 99.6 %copy-start.42 = (f32[1152]{0:T(1024)}, f32[1152]{0:T(1024)S(1)}, u32[]{:S(2)}) copy-start(f32[1152]{0:T(1024)S(1)} %subtract_convert_fusion.4) | copy-start | bytes 13828 | tf_op jit(solution)/shard_map/while
  57.6 50.0 %copy-start.20 = (bf16[640,256]{0,1:T(8,128)(2,1)}, bf16[640,256]{0,1:T(8,128)(2,1)S(1)}, u32[]{:S(2)}) copy-start(bf16[640,256]{0,1:T(8,128)(2,1)S(1)} %all_gather.65) | copy-start | bytes 983044 | tf_op jit(solution)/shard_map/while
  121.8 10.6 copy-start.25
  121.8 10.6 copy-start.27
  132.4 13.3 copy-start
  316.6 15.8 copy-start.89
  369.5 14.8 copy-start.26
  369.5 14.8 copy-start.28
  388.6 18.5 %slice-start.5 = ((s8[5242880]{0:T(1024)(128)(4,1)}), s8[1048576]{0:T(1024)(128)(4,1)S(1)}, s32[]{:S(2)}) async-start(s8[5242880]{0:T(1024)(128)(4,1)} %bitcast.325), calls=%async_computation.21 | async-start | bytes 2097152 | tf_op jit(solution)/shard_map/while
  388.6 18.5 %slice-start.11 = ((s8[4718592]{0:T(1024)(128)(4,1)}), s8[4194304]{0:T(1024)(128)(4,1)S(1)}, s32[]{:S(2)}) async-start(s8[4718592]{0:T(1024)(128)(4,1)} %bitcast.337), calls=%async_computation.27 | async-start | bytes 8388608 | tf_op jit(solution)/shard_map/while
  393.7 13.4 slice-start.6
  393.7 13.4 slice-start.12
  402.8 9.1 slice-start.7
  402.8 9.1 slice-start.9
  452.9 102.5 %all-gather.6.cloned.1.call-start = ((), (), s32[]{:S(2)}) async-start(), calls=%async_computation.11 | async-start | bytes 1351680 | tf_op jit(solution)/shard_map/while/body/eval_jaxpr/all_gather | solution.py:97
  453.4 143.1 %all-gather.8.cloned.1.call-start = ((), (), s32[]{:S(2)}) async-start(), calls=%async_computation.12 | async-start | bytes 1351680 | tf_op jit(solution)/shard_map/while/body/eval_jaxpr/all_gather | solution.py:100
  454.2 171.5 %all-gather.10.cloned.1.call-start = ((), (), s32[]{:S(2)}) async-start(), calls=%async_computation.13 | async-start | bytes 2703360 | tf_op jit(solution)/shard_map/while/body/eval_jaxpr/all_gather | solution.py:101
  454.9 230.6 %all-gather.12.cloned.1.call-start = ((), (), s32[]{:S(2)}) async-start(), calls=%async_computation.14 | async-start | bytes 2703360 | tf_op jit(solution)/shard_map/while/body/eval_jaxpr/all_gather | solution.py:102
  455.7 289.5 %all-gather.14.cloned.1.call-start = ((), (), s32[]{:S(2)}) async-start(), calls=%async_computation.15 | async-start | bytes 2703360 | tf_op jit(solution)/shard_map/while/body/eval_jaxpr/all_gather | solution.py:103
  456.3 96.4 %copy-start.81 = (f32[128]{0:T(128)}, f32[128]{0:T(128)S(1)}, u32[]{:S(2)}) copy-start(f32[128]{0:T(128)S(1)} %multiply_exponential_fusion.2) | copy-start | bytes 1540 | tf_op jit(solution)/shard_map/while
  457.3 95.4 %copy-start.42 = (f32[1152]{0:T(1024)}, f32[1152]{0:T(1024)S(1)}, u32[]{:S(2)}) copy-start(f32[1152]{0:T(1024)S(1)} %subtract_convert_fusion.4) | copy-start | bytes 13828 | tf_op jit(solution)/shard_map/while
  498.0 49.9 %copy-start.20 = (bf16[640,256]{0,1:T(8,128)(2,1)}, bf16[640,256]{0,1:T(8,128)(2,1)S(1)}, u32[]{:S(2)}) copy-start(bf16[640,256]{0,1:T(8,128)(2,1)S(1)} %all_gather.65) | copy-start | bytes 983044 | tf_op jit(solution)/shard_map/while
  562.1 10.3 copy-start.25
  562.1 10.2 copy-start.27
  572.4 13.3 copy-start
  757.0 15.7 copy-start.89
  809.6 14.8 copy-start.26
  809.6 14.8 copy-start.28
  828.8 20.3 %slice-start.5 = ((s8[5242880]{0:T(1024)(128)(4,1)}), s8[1048576]{0:T(1024)(128)(4,1)S(1)}, s32[]{:S(2)}) async-start(s8[5242880]{0:T(1024)(128)(4,1)} %bitcast.325), calls=%async_computation.21 | async-start | bytes 2097152 | tf_op jit(solution)/shard_map/while
  828.8 20.3 %slice-start.11 = ((s8[4718592]{0:T(1024)(128)(4,1)}), s8[4194304]{0:T(1024)(128)(4,1)S(1)}, s32[]{:S(2)}) async-start(s8[4718592]{0:T(1024)(128)(4,1)} %bitcast.337), calls=%async_computation.27 | async-start | bytes 8388608 | tf_op jit(solution)/shard_map/while
  834.1 10.6 copy-start.44
  834.1 10.6 copy-start.95
  834.1 15.0 slice-start.6
  834.1 15.0 slice-start.12
  844.7 9.1 slice-start.7
  844.7 9.1 slice-start.9
  898.4 136.4 %all-reduce.10.cloned.1.call-start = ((), (), s32[]{:S(2)}) async-start(), calls=%async_computation.10 | async-start | bytes 2621440
  903.0 270.8 %reduce-scatter.8.cloned.1.call-start = ((), (), s32[]{:S(2)}) async-start(), calls=%async_computation.6 | async-start | bytes 2703360 | tf_op jit(solution)/shard_map/reduce_scatter | solution.py:241
  903.6 406.2 %reduce-scatter.6.cloned.1.call-start = ((), (), s32[]{:S(2)}) async-start(), calls=%async_computation.5 | async-start | bytes 2703360 | tf_op jit(solution)/shard_map/reduce_scatter | solution.py:238
  905.8 546.1 %reduce-scatter.14.cloned.1.call-start = ((), (), s32[]{:S(2)}) async-start(), calls=%async_computation.9 | async-start | bytes 5406720 | tf_op jit(solution)/shard_map/reduce_scatter | solution.py:244
  906.5 687.3 %reduce-scatter.10.cloned.1.call-start = ((), (), s32[]{:S(2)}) async-start(), calls=%async_computation.7 | async-start | bytes 5406720 | tf_op jit(solution)/shard_map/reduce_scatter | solution.py:242
  912.5 823.3 %reduce-scatter.12.cloned.1.call-start = ((), (), s32[]{:S(2)}) async-start(), calls=%async_computation.8 | async-start | bytes 5406720 | tf_op jit(solution)/shard_map/reduce_scatter | solution.py:243
  (179 other events, 586.2 us)
Sparse Core Ops, SparseCore 0:
  12.1 57.3 all-gather.5
  72.3 53.2 all-gather.7
  128.5 56.9 all-gather.9
  188.2 56.8 all-gather.11
  247.9 56.8 all-gather.13
  456.2 53.5 all-gather.5
  512.6 53.1 all-gather.7
  568.7 56.9 all-gather.9
  628.6 56.8 all-gather.11
  688.3 56.8 all-gather.13
Sparse Core Ops, SparseCore 1:
  904.4 130.3 all-reduce.9
  1037.5 136.2 reduce-scatter.7
  1176.5 133.3 reduce-scatter.5
  1312.7 139.1 reduce-scatter.13
  1454.7 139.0 reduce-scatter.9
  1596.7 139.0 reduce-scatter.11
where the time goes:
time: 1750 us; the launch traced here: 1740 us
  waiting for transfers between devices  1020 us (58%)
  matrix products  283 us (16%)
  blocking collectives  205 us (12%)
  other arithmetic  113 us (6%)
  local copies, waits for them, and re-layouts  97.6 us (6%)
    dot_general x40, matrix products, product(): return jnp.einsum(form, left, right, preferred_element_type=jnp.float32)  204 us
    reduce_scatter x1, waiting for transfers between devices, body(): lax.psum_scatter(sums[6], ('dp', 'fsdp'), scatter_dimension=0, tiled=True)  142 us
    reduce_scatter x1, waiting for transfers between devices, body(): lax.psum_scatter(sums[4], ('dp', 'fsdp'), scatter_dimension=1, tiled=True)  142 us
    reduce_scatter x1, waiting for transfers between devices, body(): lax.psum_scatter(sums[5], ('dp', 'fsdp'), scatter_dimension=1, tiled=True)  142 us
    reduce_scatter x1, waiting for transfers between devices, body(): lax.psum_scatter(sums[3], ('dp', 'fsdp'), scatter_dimension=0, tiled=True)  138 us
    reduce_scatter x1, waiting for transfers between devices, body(): lax.psum_scatter(sums[0], ('dp', 'fsdp'), scatter_dimension=1, tiled=True)  136 us
    all_gather x2, waiting for transfers between devices, micro_step(): lax.all_gather(w_up, ('dp', 'fsdp'), axis=1, tiled=True)  100 us
    all_gather x2, waiting for transfers between devices, micro_step(): lax.all_gather(w_down, ('dp', 'fsdp'), axis=0, tiled=True)  94.6 us
  transfers between devices with their start and end apart: 16, of which 12 were waited for; matrix products, arithmetic and copies ran while one was open for 10% of the time, Pallas kernels for 0%

commit v1 on v0

v1 whole, which is shorter than its diff:
```python
import functools
import math

import jax
import jax.numpy as jnp
from jax import lax
from jax.sharding import PartitionSpec as P

HQ = 4
HD = 256
WINDOW = 512
AXES = ("dp", "fsdp")
epsilon = 1e-06


def rms_scale(values, scale_gain):
    return (
        values * lax.rsqrt(jnp.mean(values * values, axis=-1, keepdims=True) + epsilon) * scale_gain
    )


def rotate(values, angles):
    half_size = values.shape[-1] // 2
    cos_part = jnp.cos(angles)[:, None, :]
    sin_part = jnp.sin(angles)[:, None, :]
    leading = values[..., :half_size]
    trailing = values[..., half_size:]
    return jnp.concatenate(
        [leading * cos_part - trailing * sin_part, trailing * cos_part + leading * sin_part],
        axis=-1,
    )


def layout(doc_lengths, row_count, window_size, head_size):
    places = jnp.arange(row_count, dtype=jnp.int32)
    doc_ends = jnp.cumsum(doc_lengths)
    passed = places[:, None] >= doc_ends[None, :]
    doc_index = jnp.sum(passed.astype(jnp.int32), axis=1)
    doc_start = jnp.sum(jnp.where(passed, doc_lengths[None, :], 0), axis=1)
    position = (places - doc_start).astype(jnp.float32)
    steps_back = places[:, None] - places[None, :]
    visible = (
        (doc_index[:, None] == doc_index[None, :]) & (steps_back >= 0) & (steps_back < window_size)
    )
    frequency = jnp.exp(
        jnp.arange(head_size // 2, dtype=jnp.float32) * (-2.0 * math.log(10000.0) / head_size)
    )
    angles = position[:, None] * frequency[None, :]
    return (angles, visible)


def head_prep(query_raw, key_raw, gain_query, gain_key, angles):
    row_count = query_raw.shape[0]
    queries = rotate(rms_scale(query_raw.reshape(row_count, HQ, HD), gain_query), angles)
    keys_rot = rotate(rms_scale(key_raw[:, None, :], gain_key), angles)[:, 0, :]
    return (queries, keys_rot)


def gelu_product(gate_pre, up_pre):
    return jax.nn.gelu(gate_pre, approximate=True) * up_pre


def product(form, left, right):
    return jnp.einsum(form, left, right, preferred_element_type=jnp.float32)


def swap(x, bit, count):
    return lax.ppermute(x, AXES, [(i, i ^ bit) for i in range(count)])


def bit_orders(count):
    bits = [1 << k for k in range(count.bit_length() - 1)]
    middle = bits[1:-1][::-1]
    orders = []
    for turn in range(3):
        turn %= max(len(middle), 1)
        orders.append([bits[-1]] + middle[turn:] + middle[:turn] + [bits[0]])
    return orders


def gather_relative(x, order, count):
    for bit in order:
        x = jnp.concatenate([x, swap(x, bit, count)], axis=0)
    return x


def gather_absolute(x, order, count, me):
    held = []
    for bit in order:
        other = swap(x, bit, count)
        mine_second = (me & bit) != 0
        axis = sum(1 for b in held if b > bit)
        x = jnp.stack(
            [jnp.where(mine_second, other, x), jnp.where(mine_second, x, other)], axis=axis
        )
        held.append(bit)
    return x.reshape((count,) + x.shape[len(order) :])


def places_of(order):
    count = 1 << len(order)
    return [sum(((m // bit) & 1) << k for k, bit in enumerate(order)) for m in range(count)]


def reorder(x, order_from, order_to, rows):
    n = len(order_from)
    y = x.reshape((2,) * n + (rows, x.shape[-1]))
    axes = [order_from[::-1].index(bit) for bit in order_to[::-1]]
    return y.transpose(axes + [n, n + 1]).reshape(x.shape)


def scatter_relative(x, order, count):
    for bit in order[::-1]:
        half = x.shape[0] // 2
        other = swap(x[half:], bit, count)
        total = x[:half].astype(jnp.float32) + other.astype(jnp.float32)
        x = total.astype(jnp.bfloat16) if bit != order[0] else total
    return x


def scatter_absolute(x, order, count, me):
    n = len(order)
    held = sorted(order)[::-1]
    x = x.reshape((2,) * n + x.shape[1:])
    for bit in order[::-1]:
        axis = held.index(bit)
        mine = ((me & bit) != 0).astype(jnp.int32)
        keep = lax.dynamic_index_in_dim(x, mine, axis, keepdims=False)
        send = lax.dynamic_index_in_dim(x, 1 - mine, axis, keepdims=False)
        held.remove(bit)
        total = keep.astype(jnp.float32) + swap(send, bit, count).astype(jnp.float32)
        x = total.astype(jnp.bfloat16) if bit != order[0] else total
    return x


def sum_everywhere(x, count):
    for k in range(count.bit_length() - 1):
        x = x + swap(x, 1 << k, count)
    return x


def body(
    tokens,
    cotangent,
    lengths,
    w_query,
    w_key,
    w_value,
    w_out,
    w_gate,
    w_up,
    w_down,
    gain_pre_attn,
    gain_query,
    gain_key,
    gain_post_attn,
    gain_pre_ff,
    gain_post_ff,
):
    micro_count = lengths.shape[0]
    row_count = tokens.shape[0] // micro_count
    width = tokens.shape[1]
    scale_factor = HD ** (-0.5)
    count = lax.axis_size(AXES)
    me = lax.axis_index(AXES)
    orders = bit_orders(count)
    q_rows, k_rows, o_rows, f_rows = (
        w_query.shape[1],
        w_key.shape[1],
        w_out.shape[0],
        w_gate.shape[1],
    )

    attn_shard = jnp.concatenate([w_query.T, w_key.T, w_value.T], axis=0)
    attn_all = gather_absolute(attn_shard, orders[0], count, me)
    full_query = attn_all[:, :q_rows].reshape(count * q_rows, width)
    full_key = attn_all[:, q_rows : q_rows + k_rows].reshape(count * k_rows, width)
    full_value = attn_all[:, q_rows + k_rows :].reshape(count * k_rows, width)
    full_out = gather_absolute(w_out, orders[1], count, me).reshape(count * o_rows, width)
    full_gate = gather_relative(w_gate.T, orders[0], count)
    full_up = reorder(gather_relative(w_up.T, orders[1], count), orders[1], orders[0], f_rows)
    full_down = reorder(gather_relative(w_down, orders[2], count), orders[2], orders[0], f_rows)

    source_f = tokens.astype(jnp.float32)
    upstream = cotangent.astype(jnp.float32)
    normed, back_pre_attn = jax.vjp(rms_scale, source_f, gain_pre_attn)
    normed_b = normed.astype(jnp.bfloat16)
    query_raw = product("rd,kd->rk", normed_b, full_query)
    key_raw = product("rd,kd->rk", normed_b, full_key)
    value_b = product("rd,kd->rk", normed_b, full_value).astype(jnp.bfloat16)

    kept = []
    contexts = []
    for m in range(micro_count):
        rows = slice(m * row_count, (m + 1) * row_count)
        angles, visible = layout(lengths[m], row_count, WINDOW, HD)
        (queries, keys_rot), back_heads = jax.vjp(
            lambda q, k, a, b: head_prep(q, k, a, b, angles),
            query_raw[rows],
            key_raw[rows],
            gain_query,
            gain_key,
        )
        queries_b = queries.astype(jnp.bfloat16)
        keys_b = keys_rot.astype(jnp.bfloat16)
        scores = product("rhd,cd->hrc", queries_b, keys_b) * scale_factor
        scores = jnp.where(visible[None], scores, -1e30)
        row_max = jnp.max(scores, axis=-1, keepdims=True)
        exponent = jnp.exp(scores - row_max)
        row_sum = jnp.sum(exponent, axis=-1, keepdims=True)
        attention_b = (exponent / row_sum).astype(jnp.bfloat16)
        context_b = product("hrc,cd->rhd", attention_b, value_b[rows]).astype(jnp.bfloat16)
        contexts.append(context_b.reshape(row_count, HQ * HD))
        kept.append((queries_b, keys_b, attention_b, back_heads))
    context_b = jnp.concatenate(contexts, axis=0)

    branch = product("rk,kd->rd", context_b, full_out)
    branch_normed, back_post_attn = jax.vjp(rms_scale, branch, gain_post_attn)
    middle = source_f + branch_normed
    normed_ff, back_pre_ff = jax.vjp(rms_scale, middle, gain_pre_ff)
    normed_ff_b = normed_ff.astype(jnp.bfloat16)
    gate_pre = product("rd,fd->rf", normed_ff_b, full_gate)
    up_pre = product("rd,fd->rf", normed_ff_b, full_up)
    hidden, back_gelu = jax.vjp(gelu_product, gate_pre, up_pre)
    hidden_b = hidden.astype(jnp.bfloat16)
    down_out = product("rf,fd->rd", hidden_b, full_down)
    down_normed, back_post_ff = jax.vjp(rms_scale, down_out, gain_post_ff)
    result = (middle + down_normed).astype(jnp.bfloat16)

    d_down, d_gain_post_ff = back_post_ff(upstream)
    d_down_b = d_down.astype(jnp.bfloat16)
    d_hidden = product("rd,fd->rf", d_down_b, full_down)
    d_gate, d_up = back_gelu(d_hidden)
    d_gate_b = d_gate.astype(jnp.bfloat16)
    d_up_b = d_up.astype(jnp.bfloat16)
    part_down = product("rf,rd->fd", hidden_b, d_down_b).astype(jnp.bfloat16)
    part_gate = product("rf,rd->fd", d_gate_b, normed_ff_b).astype(jnp.bfloat16)
    part_up = product("rf,rd->fd", d_up_b, normed_ff_b).astype(jnp.bfloat16)
    grad_gate = scatter_relative(part_gate, orders[0], count).T
    grad_up = scatter_relative(reorder(part_up, orders[0], orders[1], f_rows), orders[1], count).T
    grad_down = scatter_relative(reorder(part_down, orders[0], orders[2], f_rows), orders[2], count)

    d_normed_ff = product("rf,fd->rd", d_gate_b, full_gate) + product(
        "rf,fd->rd", d_up_b, full_up
    )
    d_middle_part, d_gain_pre_ff = back_pre_ff(d_normed_ff)
    d_middle = upstream + d_middle_part
    d_branch, d_gain_post_attn = back_post_attn(d_middle)
    d_branch_b = d_branch.astype(jnp.bfloat16)
    part_out = product("rk,rd->kd", context_b, d_branch_b).astype(jnp.bfloat16)
    grad_out = scatter_absolute(part_out.reshape(count, o_rows, width), orders[1], count, me)
    d_context_b = product("rd,kd->rk", d_branch_b, full_out).astype(jnp.bfloat16)

    d_query_parts, d_key_parts, d_value_parts = [], [], []
    d_gain_query = d_gain_key = 0.0
    for m in range(micro_count):
        rows = slice(m * row_count, (m + 1) * row_count)
        queries_b, keys_b, attention_b, back_heads = kept[m]
        d_context_m = d_context_b[rows].reshape(row_count, HQ, HD)
        attention_f = attention_b.astype(jnp.float32)
        d_attention = product("rhd,cd->hrc", d_context_m, value_b[rows])
        row_dot = jnp.sum(attention_f * d_attention, axis=-1, keepdims=True)
        d_scores_b = (attention_f * (d_attention - row_dot)).astype(jnp.bfloat16)
        d_queries = product("hrc,cd->rhd", d_scores_b, keys_b) * scale_factor
        d_keys = product("hrc,rhd->cd", d_scores_b, queries_b) * scale_factor
        d_value_b = product("hrc,rhd->cd", attention_b, d_context_m).astype(jnp.bfloat16)
        d_query_raw, d_key_raw, gq, gk = back_heads((d_queries, d_keys))
        d_gain_query += gq
        d_gain_key += gk
        d_query_parts.append(d_query_raw.astype(jnp.bfloat16))
        d_key_parts.append(d_key_raw.astype(jnp.bfloat16))
        d_value_parts.append(d_value_b)
    d_query_b = jnp.concatenate(d_query_parts, axis=0)
    d_key_b = jnp.concatenate(d_key_parts, axis=0)
    d_value_b = jnp.concatenate(d_value_parts, axis=0)
    part_query = product("rk,rd->kd", d_query_b, normed_b).astype(jnp.bfloat16)
    part_key = product("rk,rd->kd", d_key_b, normed_b).astype(jnp.bfloat16)
    part_value = product("rk,rd->kd", d_value_b, normed_b).astype(jnp.bfloat16)
    attn_part = jnp.concatenate(
        [
            part_query.reshape(count, q_rows, width),
            part_key.reshape(count, k_rows, width),
            part_value.reshape(count, k_rows, width),
        ],
        axis=1,
    )
    attn_grad = scatter_absolute(attn_part, orders[0], count, me)
    grad_query = attn_grad[:q_rows].T
    grad_key = attn_grad[q_rows : q_rows + k_rows].T
    grad_value = attn_grad[q_rows + k_rows :].T
    d_normed = (
        product("rk,kd->rd", d_query_b, full_query)
        + product("rk,kd->rd", d_key_b, full_key)
        + product("rk,kd->rd", d_value_b, full_value)
    )
    d_source_part, d_gain_pre_attn = back_pre_attn(d_normed)
    grad_source = d_middle + d_source_part

    gains = (
        d_gain_pre_attn,
        d_gain_query,
        d_gain_key,
        d_gain_post_attn,
        d_gain_pre_ff,
        d_gain_post_ff,
    )
    sizes = [g.shape[0] for g in gains]
    total = sum_everywhere(jnp.concatenate(gains).reshape(-1, 128), count).reshape(-1)
    gain_sums = []
    at = 0
    for size in sizes:
        gain_sums.append(total[at : at + size])
        at += size
    return (
        result,
        grad_source,
        grad_query,
        grad_key,
        grad_value,
        grad_out,
        grad_gate,
        grad_up,
        grad_down,
        *gain_sums,
    )


def solution(mesh):
    rows = P(("dp", "fsdp"), None)
    columns = P(None, ("dp", "fsdp"))
    return jax.shard_map(
        body,
        mesh=mesh,
        in_specs=(rows, rows, rows, columns, columns, columns, rows, columns, columns, rows)
        + (P(),) * 6,
        out_specs=(rows, rows, columns, columns, columns, rows, columns, columns, rows)
        + (P(),) * 6,
        check_vma=False,
    )
```

time: 1750 us -> 647 us (0.37)
  waiting for transfers between devices: 1020 us -> 53.8 us
  blocking collectives: 205 us -> 0 us
  starting transfers between devices: 0.67 us -> 65.7 us
  other arithmetic: 113 us -> 154 us
    reduce_scatter x5 -> x0, waiting for transfers between devices: 700 us -> none  [the longest x1 142 us: body(): lax.psum_scatter(sums[6], ('dp', 'fsdp'), scatter_dimension=0, tiled=True)]
    all_gather x10 -> x0, waiting for transfers between devices: 238 us -> none  [the longest x2 100 us: micro_step(): lax.all_gather(w_up, ('dp', 'fsdp'), axis=1, tiled=True)]
    all_gather x4 -> x0, blocking collectives: 166 us -> none  [the longest x2 85.4 us: micro_step(): lax.all_gather(w_value, ('dp', 'fsdp'), axis=1, tiled=True)]
    dot_general x14 -> x0, matrix products: 79.2 us -> none  [the longest x2 24.7 us: micro_step(): up_pre = jnp.dot(normed_ff_b, full_up, preferred_element_type=jnp.float32)]
    unnamed x7 -> x0, waiting for transfers between devices: 78 us -> none
    ppermute x0 -> x55, starting transfers between devices: none -> 65.7 us  [swap(): return lax.ppermute(x, AXES, [(i, i ^ bit) for i in range(count)])]
    while x413 -> x0, local copies, waits for them, and re-layouts: 62.4 us -> none
    ppermute x0 -> x55, waiting for transfers between devices: none -> 53.8 us  [swap(): return lax.ppermute(x, AXES, [(i, i ^ bit) for i in range(count)])]
  transfers between devices with their start and end apart: 16 -> 55, of which waited for: 12 -> 22; matrix products, arithmetic and copies ran while one was open for 10% -> 32% of each run, Pallas kernels for 0% -> 0%
where the time goes in v1:
time: 647 us; the launch traced here: 636 us
  matrix products  269 us (42%)
  other arithmetic  154 us (24%)
  local copies, waits for them, and re-layouts  91.4 us (14%)
  starting transfers between devices  65.7 us (10%)
  waiting for transfers between devices  53.8 us (8%)
    dot_general x31, matrix products, product(): return jnp.einsum(form, left, right, preferred_element_type=jnp.float32)  239 us
    ppermute x55, starting transfers between devices, swap(): return lax.ppermute(x, AXES, [(i, i ^ bit) for i in range(count)])  65.7 us
    ppermute x55, waiting for transfers between devices, swap(): return lax.ppermute(x, AXES, [(i, i ^ bit) for i in range(count)])  53.8 us
    unnamed x280, local copies, waits for them, and re-layouts  44.3 us
    sub x2, matrix products, body(): exponent = jnp.exp(scores - row_max)  29.5 us
    convert_element_type x2, other arithmetic, body(): d_scores_b = (attention_f * (d_attention - row_dot)).astype(jnp.bfloat16)  28.3 us
    convert_element_type x2, other arithmetic, body(): attention_b = (exponent / row_sum).astype(jnp.bfloat16)  17.7 us
    reduce_sum x4, other arithmetic, rms_scale(): values * lax.rsqrt(jnp.mean(values * values, axis=-1, keepdims=True) + ep...  13.2 us
  transfers between devices with their start and end apart: 55, of which 22 were waited for; matrix products, arithmetic and copies ran while one was open for 32% of the time, Pallas kernels for 0%

profile of v1, /device:TPU:0, one launch (start us, length us, event | category | flops | bytes accessed | tf_op | source)
XLA Modules:
  0.0 636.3 jit_solution(1631749230058174667)
XLA Ops:
  0.6 4.1 collective-permute-start.5
  19.8 3.9 copy.173
  27.9 5.6 multiply_cosine_fusion.2
  34.3 5.9 copy.192
  82.9 9.6 %collective-permute-done.13 = bf16[512,640]{1,0:T(8,128)(2,1)S(1)} collective-permute-done((bf16[512,640]{1,0:T(8,128)(2,1)S(1)}, bf16[512,640]{1,0:T(8,128)(2,1)S(1)}, u32[]{:S(2)}, u32[]{:S(2)}) %collective-permute-start.13) | collective-permute-done | bytes 655392 | tf_op jit(solution)/shard_map/ppermute | solution.py:68
  98.7 4.0 fusion.140
  102.7 4.3 fusion.143
  113.4 6.1 copy.178
  119.5 6.3 copy.182
  130.7 5.8 fusion.88
  141.9 14.5 %fusion.147 = (f32[4,1152]{1,0:T(4,128)S(1)}, f32[4,1152,1152]{1,2,0:T(8,128)}) fusion(pred[1152,1152]{0,1:T(8,128)(4,1)} %fusion.38, bf16[1152,4,128]{2,0,1:T(8,128)(2,1)} %get-tuple-element.117, bf16[1152,4,128]{2,0,1:T(8,128)(2,1)} %get-tuple-element.116, bf16[1152,1,128]{0,2,1:T(8,128)(2,1)} %get-tuple-element.214, ...), kind=kOutput, calls=%fused_computation.407 | convolution fusion | flops 2745041920 | bytes 25528320 | tf_op jit(solution)/shard_map/sub | solution.py:209
  156.5 9.4 %divide_convert_fusion = bf16[4,1152,1152]{1,2,0:T(8,128)(2,1)S(1)} fusion(f32[4,1152,1152]{1,2,0:T(8,128)} %get-tuple-element.219, f32[4,1152]{1,0:T(4,128)S(1)} %get-tuple-element.218), kind=kLoop, calls=%fused_computation.24 | loop fusion | flops 10616832 | bytes 31868928 | tf_op jit(solution)/shard_map/convert_element_type | solution.py:211
  166.0 4.6 convolution_convert_fusion.2
  172.7 15.0 %fusion.148 = (f32[4,1152]{1,0:T(4,128)}, f32[4,1152,1152]{1,2,0:T(8,128)}) fusion(pred[1152,1152]{0,1:T(8,128)(4,1)} %fusion.39, bf16[1152,4,128]{2,0,1:T(8,128)(2,1)} %get-tuple-element.115, bf16[1152,4,128]{2,0,1:T(8,128)(2,1)} %get-tuple-element.114, bf16[1152,1,128]{0,2,1:T(8,128)(2,1)S(1)} %copy-done.59, bf16[1152,1,128]{0,2,1:T(8,128)(2,1)S(1)} %copy-done.57), kind=kOutput, calls=%fused_computation.408 | convolution fusion | flops 2745041920 | bytes 25528320 | tf_op jit(solution)/shard_map/sub | solution.py:209
  187.7 8.2 %divide_convert_fusion.1 = bf16[4,1152,1152]{1,2,0:T(8,128)(2,1)S(1)} fusion(f32[4,1152,1152]{1,2,0:T(8,128)} %get-tuple-element.221, f32[4,1152]{1,0:T(4,128)} %get-tuple-element.220), kind=kLoop, calls=%fused_computation.25 | loop fusion | flops 10616832 | bytes 31868928 | tf_op jit(solution)/shard_map/convert_element_type | solution.py:211
  220.7 10.7 %fusion.149 = f32[2304,2048]{1,0:T(8,128)} fusion(bf16[2304,640]{0,1:T(8,128)(2,1)S(1)} %multiply_convert_fusion.2, bf16[2048,640]{1,0:T(8,128)(2,1)S(1)} %constant_dynamic-update-slice_fusion.5), kind=kOutput, calls=%fused_computation.409 | convolution fusion | flops 6039797760 | bytes 24444928 | tf_op jit(solution)/shard_map/rd,fd->rf/dot_general | solution.py:64
  231.4 22.5 %multiply_convert_fusion.1 = (bf16[2304,2048]{1,0:T(8,128)(2,1)}, f32[2304,2048]{1,0:T(8,128)}) fusion(f32[2304,2048]{1,0:T(8,128)} %fusion.149, bf16[2304,640]{0,1:T(8,128)(2,1)S(1)} %multiply_convert_fusion.2, bf16[2048,640]{1,0:T(8,128)(2,1)} %bitcast.399), kind=kOutput, calls=%fused_computation.34 | convolution fusion | flops 6086983680 | bytes 52756480 | tf_op jit(solution)/shard_map/rd,fd->rf/dot_general | solution.py:64
  253.9 9.9 %multiply_reduce_fusion.4 = (f32[2304]{0:T(1024)S(1)}, f32[2304,640]{0,1:T(8,128)S(1)}) fusion(bf16[2304,2048]{1,0:T(8,128)(2,1)} %get-tuple-element.224, bf16[2048,640]{1,0:T(8,128)(2,1)} %bitcast.401), kind=kOutput, calls=%fused_computation.69 | convolution fusion | flops 6042744832 | bytes 17966080 | tf_op jit(solution)/shard_map/rf,fd->rd/dot_general | solution.py:64
  266.2 5.8 fusion.29
  272.0 31.4 %fusion.20 = (bf16[2304,2048]{1,0:T(8,128)(2,1)}, bf16[2304,2048]{1,0:T(8,128)(2,1)}) fusion(f32[2304,2048]{1,0:T(8,128)} %fusion.149, f32[2304,2048]{1,0:T(8,128)} %get-tuple-element.225, bf16[2304,640]{0,1:T(8,128)(2,1)} %get-tuple-element.108, bf16[2048,640]{1,0:T(8,128)(2,1)} %bitcast.402), kind=kOutput, calls=%fused_computation.32 | convolution fusion | flops 6153043968 | bytes 62193664 | tf_op jit(solution)/shard_map/rd,fd->rf/dot_general | solution.py:64
  303.4 12.1 %fusion.150 = f32[2304,640]{0,1:T(8,128)} fusion(bf16[2304,2048]{1,0:T(8,128)(2,1)} %get-tuple-element.105, bf16[2048,640]{1,0:T(8,128)(2,1)} %bitcast.400), kind=kOutput, calls=%fused_computation.410 | convolution fusion | flops 6039797760 | bytes 17956864 | tf_op jit(solution)/shard_map/rf,fd->rd/dot_general | solution.py:64
  315.5 16.4 %multiply_reduce_fusion = (f32[640]{0:T(1024)}, f32[2304]{0:T(1024)S(1)}, f32[2304,640]{0,1:T(8,128)}) fusion(f32[2304,640]{0,1:T(8,128)} %copy-done, f32[2304]{0:T(1024)S(1)} %fusion.110, f32[640]{0:T(1024)S(1)} %copy-done.94, f32[2304,640]{0,1:T(8,128)} %fusion.150, bf16[2304,2048]{1,0:T(8,128)(2,1)} %get-tuple-element.104, bf16[2048,640]{1,0:T(8,128)(2,1)} %copy-done.107), kind=kOutput, calls=%fused_computation.63 | convolution fusion | flops 6050116608 | bytes 29776896 | tf_op jit(solution)/shard_map/rf,fd->rd/dot_general | solution.py:64
  332.0 6.7 %multiply_reduce_fusion.1 = (f32[640]{0:T(1024)}, f32[2304]{0:T(1024)S(1)}, f32[2304,640]{0,1:T(8,128)S(1)}) fusion(f32[2304,640]{0,1:T(8,128)} %copy-done.5, f32[2304]{0:T(1024)S(1)} %copy-done.64, f32[640]{0:T(1024)S(1)} %copy-done.92, f32[2304,640]{0,1:T(8,128)S(1)} %bitcast.369, f32[2304]{0:T(1024)S(1)} %multiply_multiply_fusion.9, ...), kind=kLoop, calls=%fused_computation.64 | loop fusion | flops 19166336 | bytes 26586624 | tf_op jit(solution)/shard_map/transpose(jvp())/reduce_sum | solution.py:18
  338.7 8.1 %fusion.30 = bf16[2304,640]{0,1:T(8,128)(2,1)} fusion(f32[2304,640]{0,1:T(8,128)} %copy-done.5, f32[2304,640]{0,1:T(8,128)S(1)} %get-tuple-element.101, f32[2304]{0:T(1024)S(1)} %multiply_multiply_fusion.8, f32[640]{0:T(1024)S(1)} %copy-done.92, f32[2304]{0:T(1024)S(1)} %copy-done.64), kind=kLoop, calls=%fused_computation.59 | loop fusion | flops 8847360 | bytes 14766592 | tf_op jit(solution)/shard_map/convert_element_type | solution.py:249
  346.8 6.1 convolution_convert_fusion
  360.1 12.7 %fusion.10 = (f32[4,1152]{1,0:T(4,128)S(1)}, f32[4,1152,1152]{1,2,0:T(8,128)}) fusion(bf16[4,1152,1152]{1,2,0:T(8,128)(2,1)} %copy-done.8, bf16[1152,4,256]{0,2,1:T(8,128)(2,1)} %bitcast.389, bf16[2304,256]{1,0:T(8,128)(2,1)S(1)} %copy-done.50), kind=kOutput, calls=%fused_computation.20 | convolution fusion | flops 2733829632 | bytes 34818048 | tf_op jit(solution)/shard_map/rhd,cd->hrc/dot_general | solution.py:64
  372.8 3.8 fusion.55
  376.6 8.7 %fusion.12 = (f32[4,1152]{1,0:T(4,128)S(1)}, f32[4,1152,1152]{1,2,0:T(8,128)}) fusion(bf16[4,1152,1152]{1,2,0:T(8,128)(2,1)S(1)} %bitcast.379, bf16[1152,4,256]{0,2,1:T(8,128)(2,1)S(1)} %bitcast.387, bf16[2304,256]{1,0:T(8,128)(2,1)S(1)} %copy-done.50), kind=kOutput, calls=%fused_computation.22 | convolution fusion | flops 2733829632 | bytes 34818048 | tf_op jit(solution)/shard_map/rhd,cd->hrc/dot_general | solution.py:64
  385.3 14.1 %fusion.13 = bf16[4,1152,1152]{1,2,0:T(8,128)(2,1)S(1)} fusion(f32[4,1152,1152]{1,2,0:T(8,128)} %get-tuple-element.232, f32[4,1152]{1,0:T(4,128)S(1)} %get-tuple-element.231, f32[4,1152,1152]{1,2,0:T(8,128)} %get-tuple-element.219, f32[4,1152]{1,0:T(4,128)S(1)} %copy-done.82), kind=kLoop, calls=%fused_computation.23 | loop fusion | flops 31850496 | bytes 53121024 | tf_op jit(solution)/shard_map/convert_element_type | solution.py:263
  399.5 6.1 fusion.43
  409.1 14.2 %fusion.11 = bf16[4,1152,1152]{1,2,0:T(8,128)(2,1)S(1)} fusion(f32[4,1152,1152]{1,2,0:T(8,128)} %get-tuple-element.230, f32[4,1152]{1,0:T(4,128)S(1)} %get-tuple-element.229, f32[4,1152,1152]{1,2,0:T(8,128)} %get-tuple-element.221, f32[4,1152]{1,0:T(4,128)S(1)} %copy-done.83), kind=kLoop, calls=%fused_computation.21 | loop fusion | flops 31850496 | bytes 53121024 | tf_op jit(solution)/shard_map/convert_element_type | solution.py:263
  423.3 6.1 fusion.42
  429.4 4.5 fusion.51
  444.5 5.4 fusion.40
  450.0 4.3 copy.206
  457.2 6.4 %fusion.45 = f32[2304,640]{0,1:T(8,128)S(1)} fusion(bf16[1024,640]{1,0:T(8,128)(2,1)} %bitcast.416, bf16[1152,1024]{0,1:T(8,128)(2,1)} %bitcast.403, bf16[1152,1024]{0,1:T(8,128)(2,1)} %bitcast.405), kind=kOutput, calls=%fused_computation.107 | convolution fusion | flops 3029336064 | bytes 11927552 | tf_op jit(solution)/shard_map/rk,kd->rd/dot_general | solution.py:64
  463.8 4.0 fusion.58
  467.8 3.9 fusion.57
  471.6 11.3 %convolution_convert_fusion.6 = bf16[2048,640]{1,0:T(8,128)(2,1)} fusion(bf16[2304,2048]{1,0:T(8,128)(2,1)} %get-tuple-element.104, bf16[2304,640]{0,1:T(8,128)(2,1)S(1)} %copy-done.26), kind=kOutput, calls=%fused_computation.105 | convolution fusion | flops 6041108480 | bytes 15007744 | tf_op jit(solution)/shard_map/rf,rd->fd/dot_general | solution.py:64
  482.9 11.8 %convolution_convert_fusion.5 = bf16[2048,640]{1,0:T(8,128)(2,1)} fusion(bf16[2304,2048]{1,0:T(8,128)(2,1)} %get-tuple-element.105, bf16[2304,640]{0,1:T(8,128)(2,1)S(1)} %copy-done.26), kind=kOutput, calls=%fused_computation.104 | convolution fusion | flops 6041108480 | bytes 15007744 | tf_op jit(solution)/shard_map/rf,rd->fd/dot_general | solution.py:64
  494.8 11.3 %convolution_convert_fusion.4 = bf16[2048,640]{1,0:T(8,128)(2,1)} fusion(bf16[2304,2048]{1,0:T(8,128)(2,1)} %get-tuple-element.224, bf16[2304,640]{0,1:T(8,128)(2,1)S(1)} %copy-done.24), kind=kOutput, calls=%fused_computation.103 | convolution fusion | flops 6041108480 | bytes 15007744 | tf_op jit(solution)/shard_map/rf,rd->fd/dot_general | solution.py:64
  506.1 4.9 fusion.97
  515.7 6.8 %fusion.26 = (f32[640]{0:T(1024)S(1)}, f32[2304]{0:T(1024)S(1)}, f32[2304,640]{0,1:T(8,128)}) fusion(bf16[2304,640]{0,1:T(8,128)(2,1)S(1)} %copy-done.3, f32[2304]{0:T(1024)S(1)} %copy-done.76, f32[640]{0:T(1024)S(1)} %copy-done.98, bf16[32,48,640]{2,1,0:T(8,128)(2,1)} %bitcast.394, bf16[1152,256]{1,0:T(8,128)(2,1)S(1)} %copy-done.52, ...), kind=kOutput, calls=%fused_computation.55 | convolution fusion | flops 770602112 | bytes 22174720 | tf_op jit(solution)/shard_map/rk,kd->rd/dot_general | solution.py:64
  525.2 6.8 %fusion.31 = f32[2304,640]{0,1:T(8,128)} fusion(f32[2304,640]{0,1:T(8,128)S(1)} %bitcast.377, bf16[2304,640]{0,1:T(8,128)(2,1)S(1)} %copy-done.3, f32[2304,640]{0,1:T(8,128)} %get-tuple-element.233, f32[2304]{0:T(1024)S(1)} %multiply_multiply_fusion.7, f32[640]{0:T(1024)S(1)} %copy-done.98, f32[2304]{0:T(1024)S(1)} %copy-done.76), kind=kLoop, calls=%fused_computation.60 | loop fusion | flops 10321920 | bytes 20664832 | tf_op jit(solution)/shard_map/add | solution.py:297
  543.2 7.9 %copy.224 = f32[2304,640]{1,0:T(8,128)} copy(f32[2304,640]{0,1:T(8,128)} %fusion.31) | data formatting | bytes 11796480
  562.4 5.3 collective-permute-done.31
  569.1 4.0 collective-permute-done.32
  608.7 4.1 collective-permute-done.46
  (547 shorter events, 227.7 us)
Async XLA Ops:
  0.6 39.6 %collective-permute-start.5 = (bf16[32,640]{1,0:T(8,128)(2,1)}, bf16[32,640]{1,0:T(8,128)(2,1)}, u32[]{:S(2)}, u32[]{:S(2)}) collective-permute-start(bf16[32,640]{1,0:T(8,128)(2,1)} %param.22), channel_id=1, source_target_pairs={{0,16},{1,17},{2,18},{3,19},{4,20},{5,21},{6,22},{7,23},{8,24},{9,... | collective-permute-start | bytes 122888 | tf_op jit(solution)/shard_map/ppermute | solution.py:68
  6.2 36.5 %collective-permute-start = (bf16[48,640]{1,0:T(8,128)(2,1)}, bf16[48,640]{1,0:T(8,128)(2,1)}, u32[]{:S(2)}, u32[]{:S(2)}) collective-permute-start(bf16[48,640]{1,0:T(8,128)(2,1)} %pad_maximum_fusion.50), channel_id=1, source_target_pairs={{0,16},{1,17},{2,18},{3,19},{4,20},{5,21},{6,22},{7,23},{8,24},{9,... | collective-permute-start | bytes 184328 | tf_op jit(solution)/shard_map/ppermute | solution.py:68
  6.2 39.1 %collective-permute-start.10 = (bf16[64,640]{1,0:T(8,128)(2,1)}, bf16[64,640]{1,0:T(8,128)(2,1)}, u32[]{:S(2)}, u32[]{:S(2)}) collective-permute-start(bf16[64,640]{1,0:T(8,128)(2,1)} %bitcast.407), channel_id=1, source_target_pairs={{0,16},{1,17},{2,18},{3,19},{4,20},{5,21},{6,22},{7,23},{8,24},{9,... | collective-permute-start | bytes 245768 | tf_op jit(solution)/shard_map/ppermute | solution.py:68
  9.1 37.6 %collective-permute-start.15 = (bf16[64,640]{1,0:T(8,128)(2,1)}, bf16[64,640]{1,0:T(8,128)(2,1)}, u32[]{:S(2)}, u32[]{:S(2)}) collective-permute-start(bf16[64,640]{1,0:T(8,128)(2,1)} %bitcast.411), channel_id=1, source_target_pairs={{0,16},{1,17},{2,18},{3,19},{4,20},{5,21},{6,22},{7,23},{8,24},{9,... | collective-permute-start | bytes 245768 | tf_op jit(solution)/shard_map/ppermute | solution.py:68
  9.2 39.1 %collective-permute-start.20 = (bf16[64,640]{1,0:T(8,128)(2,1)}, bf16[64,640]{1,0:T(8,128)(2,1)}, u32[]{:S(2)}, u32[]{:S(2)}) collective-permute-start(bf16[64,640]{1,0:T(8,128)(2,1)} %param.25), channel_id=1, source_target_pairs={{0,16},{1,17},{2,18},{3,19},{4,20},{5,21},{6,22},{7,23},{8,24},{9,... | collective-permute-start | bytes 245768 | tf_op jit(solution)/shard_map/ppermute | solution.py:68
  41.2 14.4 %collective-permute-start.6 = (bf16[2,32,640]{2,1,0:T(8,128)(2,1)S(1)}, bf16[2,32,640]{2,1,0:T(8,128)(2,1)S(1)}, u32[]{:S(2)}, u32[]{:S(2)}) collective-permute-start(bf16[2,32,640]{2,1,0:T(8,128)(2,1)S(1)} %pad_maximum_fusion.49), channel_id=1, source_target_pairs={{0,4},{1,5},{2,6},{3,7},{4,0},{5,1},{6,2},{7,3},{8,12},{9,13},{10,... | collective-permute-start | bytes 245768 | tf_op jit(solution)/shard_map/ppermute | solution.py:68
  43.6 12.5 %collective-permute-start.1 = (bf16[2,48,640]{2,1,0:T(8,128)(2,1)S(1)}, bf16[2,48,640]{2,1,0:T(8,128)(2,1)S(1)}, u32[]{:S(2)}, u32[]{:S(2)}) collective-permute-start(bf16[2,48,640]{2,1,0:T(8,128)(2,1)S(1)} %pad_maximum_fusion.48), channel_id=1, source_target_pairs={{0,8},{1,9},{2,10},{3,11},{4,12},{5,13},{6,14},{7,15},{8,0},{9,1},... | collective-permute-start | bytes 368648 | tf_op jit(solution)/shard_map/ppermute | solution.py:68
  46.2 11.6 %collective-permute-start.11 = (bf16[128,640]{1,0:T(8,128)(2,1)S(1)}, bf16[128,640]{1,0:T(8,128)(2,1)S(1)}, u32[]{:S(2)}, u32[]{:S(2)}) collective-permute-start(bf16[128,640]{1,0:T(8,128)(2,1)S(1)} %pad_maximum_fusion.45), channel_id=1, source_target_pairs={{0,8},{1,9},{2,10},{3,11},{4,12},{5,13},{6,14},{7,15},{8,0},{9,1},... | collective-permute-start | bytes 491528 | tf_op jit(solution)/shard_map/ppermute | solution.py:68
  47.7 11.6 %collective-permute-start.16 = (bf16[128,640]{1,0:T(8,128)(2,1)S(1)}, bf16[128,640]{1,0:T(8,128)(2,1)S(1)}, u32[]{:S(2)}, u32[]{:S(2)}) collective-permute-start(bf16[128,640]{1,0:T(8,128)(2,1)S(1)} %pad_maximum_fusion.46), channel_id=1, source_target_pairs={{0,4},{1,5},{2,6},{3,7},{4,0},{5,1},{6,2},{7,3},{8,12},{9,13},{10,... | collective-permute-start | bytes 491528 | tf_op jit(solution)/shard_map/ppermute | solution.py:68
  49.2 12.6 %collective-permute-start.21 = (bf16[128,640]{1,0:T(8,128)(2,1)S(1)}, bf16[128,640]{1,0:T(8,128)(2,1)S(1)}, u32[]{:S(2)}, u32[]{:S(2)}) collective-permute-start(bf16[128,640]{1,0:T(8,128)(2,1)S(1)} %pad_maximum_fusion.47), channel_id=1, source_target_pairs={{0,2},{1,3},{2,0},{3,1},{4,6},{5,7},{6,4},{7,5},{8,10},{9,11},{10,... | collective-permute-start | bytes 491528 | tf_op jit(solution)/shard_map/ppermute | solution.py:68
  55.6 11.1 %collective-permute-start.7 = (bf16[2,2,32,640]{3,2,1,0:T(8,128)(2,1)S(1)}, bf16[2,2,32,640]{3,2,1,0:T(8,128)(2,1)S(1)}, u32[]{:S(2)}, u32[]{:S(2)}) collective-permute-start(bf16[2,2,32,640]{3,2,1,0:T(8,128)(2,1)S(1)} %pad_maximum_fusion.44), channel_id=1, source_target_pairs={{0,2},{1,3},{2,0},{3,1},{4,6},{5,7},{6,4},{7,5},{8,10},{9,11},{10,... | collective-permute-start | bytes 491528 | tf_op jit(solution)/shard_map/ppermute | solution.py:68
  56.2 11.1 %collective-permute-start.2 = (bf16[2,2,48,640]{3,2,1,0:T(8,128)(2,1)S(1)}, bf16[2,2,48,640]{3,2,1,0:T(8,128)(2,1)S(1)}, u32[]{:S(2)}, u32[]{:S(2)}) collective-permute-start(bf16[2,2,48,640]{3,2,1,0:T(8,128)(2,1)S(1)} %pad_maximum_fusion.43), channel_id=1, source_target_pairs={{0,4},{1,5},{2,6},{3,7},{4,0},{5,1},{6,2},{7,3},{8,12},{9,13},{10,... | collective-permute-start | bytes 737288 | tf_op jit(solution)/shard_map/ppermute | solution.py:68
  58.7 9.3 %collective-permute-start.12 = (bf16[256,640]{1,0:T(8,128)(2,1)S(1)}, bf16[256,640]{1,0:T(8,128)(2,1)S(1)}, u32[]{:S(2)}, u32[]{:S(2)}) collective-permute-start(bf16[256,640]{1,0:T(8,128)(2,1)S(1)} %pad_maximum_fusion.40), channel_id=1, source_target_pairs={{0,4},{1,5},{2,6},{3,7},{4,0},{5,1},{6,2},{7,3},{8,12},{9,13},{10,... | collective-permute-start | bytes 983048 | tf_op jit(solution)/shard_map/ppermute | solution.py:68
  60.2 10.3 %collective-permute-start.17 = (bf16[256,640]{1,0:T(8,128)(2,1)S(1)}, bf16[256,640]{1,0:T(8,128)(2,1)S(1)}, u32[]{:S(2)}, u32[]{:S(2)}) collective-permute-start(bf16[256,640]{1,0:T(8,128)(2,1)S(1)} %pad_maximum_fusion.41), channel_id=1, source_target_pairs={{0,2},{1,3},{2,0},{3,1},{4,6},{5,7},{6,4},{7,5},{8,10},{9,11},{10,... | collective-permute-start | bytes 983048 | tf_op jit(solution)/shard_map/ppermute | solution.py:68
  62.8 10.7 %collective-permute-start.22 = (bf16[256,640]{1,0:T(8,128)(2,1)S(1)}, bf16[256,640]{1,0:T(8,128)(2,1)S(1)}, u32[]{:S(2)}, u32[]{:S(2)}) collective-permute-start(bf16[256,640]{1,0:T(8,128)(2,1)S(1)} %pad_maximum_fusion.42), channel_id=1, source_target_pairs={{0,8},{1,9},{2,10},{3,11},{4,12},{5,13},{6,14},{7,15},{8,0},{9,1},... | collective-permute-start | bytes 983048 | tf_op jit(solution)/shard_map/ppermute | solution.py:68
  66.8 13.7 %collective-permute-start.8 = (bf16[2,2,2,32,640]{4,3,2,1,0:T(8,128)(2,1)S(1)}, bf16[2,2,2,32,640]{4,3,2,1,0:T(8,128)(2,1)S(1)}, u32[]{:S(2)}, u32[]{:S(2)}) collective-permute-start(bf16[2,2,2,32,640]{4,3,2,1,0:T(8,128)(2,1)S(1)} %pad_maximum_fusion.39), channel_id=1, source_target_pairs={{0,8},{1,9},{2,10},{3,11},{4,12},{5,13},{6,14},{7,15},{8,0},{9,1},... | collective-permute-start | bytes 983048 | tf_op jit(solution)/shard_map/ppermute | solution.py:68
  67.4 14.2 %collective-permute-start.3 = (bf16[2,2,2,48,640]{4,3,2,1,0:T(8,128)(2,1)S(1)}, bf16[2,2,2,48,640]{4,3,2,1,0:T(8,128)(2,1)S(1)}, u32[]{:S(2)}, u32[]{:S(2)}) collective-permute-start(bf16[2,2,2,48,640]{4,3,2,1,0:T(8,128)(2,1)S(1)} %pad_maximum_fusion.38), channel_id=1, source_target_pairs={{0,2},{1,3},{2,0},{3,1},{4,6},{5,7},{6,4},{7,5},{8,10},{9,11},{10,... | collective-permute-start | bytes 1474568 | tf_op jit(solution)/shard_map/ppermute | solution.py:68
  68.9 23.5 %collective-permute-start.13 = (bf16[512,640]{1,0:T(8,128)(2,1)S(1)}, bf16[512,640]{1,0:T(8,128)(2,1)S(1)}, u32[]{:S(2)}, u32[]{:S(2)}) collective-permute-start(bf16[512,640]{1,0:T(8,128)(2,1)S(1)} %pad_maximum_fusion.35), channel_id=1, source_target_pairs={{0,2},{1,3},{2,0},{3,1},{4,6},{5,7},{6,4},{7,5},{8,10},{9,11},{10,... | collective-permute-start | bytes 1966088 | tf_op jit(solution)/shard_map/ppermute | solution.py:68
  71.5 22.1 %collective-permute-start.18 = (bf16[512,640]{1,0:T(8,128)(2,1)S(1)}, bf16[512,640]{1,0:T(8,128)(2,1)S(1)}, u32[]{:S(2)}, u32[]{:S(2)}) collective-permute-start(bf16[512,640]{1,0:T(8,128)(2,1)S(1)} %pad_maximum_fusion.36), channel_id=1, source_target_pairs={{0,8},{1,9},{2,10},{3,11},{4,12},{5,13},{6,14},{7,15},{8,0},{9,1},... | collective-permute-start | bytes 1966088 | tf_op jit(solution)/shard_map/ppermute | solution.py:68
  74.4 20.9 %collective-permute-start.23 = (bf16[512,640]{1,0:T(8,128)(2,1)S(1)}, bf16[512,640]{1,0:T(8,128)(2,1)S(1)}, u32[]{:S(2)}, u32[]{:S(2)}) collective-permute-start(bf16[512,640]{1,0:T(8,128)(2,1)S(1)} %pad_maximum_fusion.37), channel_id=1, source_target_pairs={{0,4},{1,5},{2,6},{3,7},{4,0},{5,1},{6,2},{7,3},{8,12},{9,13},{10,... | collective-permute-start | bytes 1966088 | tf_op jit(solution)/shard_map/ppermute | solution.py:68
  80.6 15.8 %collective-permute-start.9 = (bf16[2,2,2,2,32,640]{5,4,3,2,1,0:T(8,128)(2,1)S(1)}, bf16[2,2,2,2,32,640]{5,4,3,2,1,0:T(8,128)(2,1)S(1)}, u32[]{:S(2)}, u32[]{:S(2)}) collective-permute-start(bf16[2,2,2,2,32,640]{5,4,3,2,1,0:T(8,128)(2,1)S(1)} %pad_maximum_fusion.34), channel_id=1, source_target_pairs={{0,1},{1,0},{2,3},{3,2},{4,5},{5,4},{6,7},{7,6},{8,9},{9,8},{10,11... | collective-permute-start | bytes 1966088 | tf_op jit(solution)/shard_map/ppermute | solution.py:68
  81.9 15.9 %collective-permute-start.4 = (bf16[2,2,2,2,48,640]{5,4,3,2,1,0:T(8,128)(2,1)S(1)}, bf16[2,2,2,2,48,640]{5,4,3,2,1,0:T(8,128)(2,1)S(1)}, u32[]{:S(2)}, u32[]{:S(2)}) collective-permute-start(bf16[2,2,2,2,48,640]{5,4,3,2,1,0:T(8,128)(2,1)S(1)} %pad_maximum_fusion.17), channel_id=1, source_target_pairs={{0,1},{1,0},{2,3},{3,2},{4,5},{5,4},{6,7},{7,6},{8,9},{9,8},{10,11... | collective-permute-start | bytes 2949128 | tf_op jit(solution)/shard_map/ppermute | solution.py:68
  93.6 124.7 %collective-permute-start.14 = (bf16[1024,640]{1,0:T(8,128)(2,1)}, bf16[1024,640]{1,0:T(8,128)(2,1)}, u32[]{:S(2)}, u32[]{:S(2)}) collective-permute-start(bf16[1024,640]{1,0:T(8,128)(2,1)} %get-tuple-element.148), channel_id=1, source_target_pairs={{0,1},{1,0},{2,3},{3,2},{4,5},{5,4},{6,7},{7,6},{8,9},{9,8},{10,11... | collective-permute-start | bytes 3932168 | tf_op jit(solution)/shard_map/ppermute | solution.py:68
  94.8 114.8 %collective-permute-start.19 = (bf16[1024,640]{1,0:T(8,128)(2,1)}, bf16[1024,640]{1,0:T(8,128)(2,1)}, u32[]{:S(2)}, u32[]{:S(2)}) collective-permute-start(bf16[1024,640]{1,0:T(8,128)(2,1)} %get-tuple-element.150), channel_id=1, source_target_pairs={{0,1},{1,0},{2,3},{3,2},{4,5},{5,4},{6,7},{7,6},{8,9},{9,8},{10,11... | collective-permute-start | bytes 3932168 | tf_op jit(solution)/shard_map/ppermute | solution.py:68
  96.5 117.5 %collective-permute-start.24 = (bf16[1024,640]{1,0:T(8,128)(2,1)}, bf16[1024,640]{1,0:T(8,128)(2,1)}, u32[]{:S(2)}, u32[]{:S(2)}) collective-permute-start(bf16[1024,640]{1,0:T(8,128)(2,1)} %get-tuple-element.146), channel_id=1, source_target_pairs={{0,1},{1,0},{2,3},{3,2},{4,5},{5,4},{6,7},{7,6},{8,9},{9,8},{10,11... | collective-permute-start | bytes 3932168 | tf_op jit(solution)/shard_map/ppermute | solution.py:68
  524.5 32.9 %collective-permute-start.30 = (bf16[2,2,2,2,32,640]{5,4,0,2,3,1:T(8,128)(2,1)}, bf16[2,2,2,2,32,640]{5,4,0,2,3,1:T(8,128)(2,1)}, u32[]{:S(2)}, u32[]{:S(2)}) collective-permute-start(bf16[2,2,2,2,32,640]{5,4,0,2,3,1:T(8,128)(2,1)} %bitcast.367), channel_id=1, source_target_pairs={{0,1},{1,0},{2,3},{3,2},{4,5},{5,4},{6,7},{7,6},{8,9},{9,8},{10,11... | collective-permute-start | bytes 1966088 | tf_op jit(solution)/shard_map/ppermute | solution.py:68
  525.1 8.1 %collective-permute-start.50 = (f32[24,128]{1,0:T(8,128)S(1)}, f32[24,128]{1,0:T(8,128)S(1)}, u32[]{:S(2)}, u32[]{:S(2)}) collective-permute-start(f32[24,128]{1,0:T(8,128)S(1)} %bitcast.428), channel_id=1, source_target_pairs={{0,1},{1,0},{2,3},{3,2},{4,5},{5,4},{6,7},{7,6},{8,9},{9,8},{10,11... | collective-permute-start | bytes 36872 | tf_op jit(solution)/shard_map/ppermute | solution.py:68
  537.0 16.3 %collective-permute-start.52 = (f32[24,128]{1,0:T(8,128)S(1)}, f32[24,128]{1,0:T(8,128)S(1)}, u32[]{:S(2)}, u32[]{:S(2)}) collective-permute-start(f32[24,128]{1,0:T(8,128)S(1)} %fusion.187), channel_id=1, source_target_pairs={{0,4},{1,5},{2,6},{3,7},{4,0},{5,1},{6,2},{7,3},{8,12},{9,13},{10,... | collective-permute-start | bytes 36872 | tf_op jit(solution)/shard_map/ppermute | solution.py:68
  551.3 17.6 %collective-permute-start.25 = (bf16[2,2,2,2,48,640]{5,4,0,1,2,3:T(8,128)(2,1)S(1)}, bf16[2,2,2,2,48,640]{5,4,0,1,2,3:T(8,128)(2,1)S(1)}, u32[]{:S(2)}, u32[]{:S(2)}) collective-permute-start(bf16[2,2,2,2,48,640]{5,4,0,1,2,3:T(8,128)(2,1)S(1)} %bitcast.423), channel_id=1, source_target_pairs={{0,1},{1,0},{2,3},{3,2},{4,5},{5,4},{6,7},{7,6},{8,9},{9,8},{10,11... | collective-permute-start | bytes 2949128 | tf_op jit(solution)/shard_map/ppermute | solution.py:68
  552.9 33.1 %collective-permute-start.35 = (bf16[1024,640]{1,0:T(8,128)(2,1)S(1)}, bf16[1024,640]{1,0:T(8,128)(2,1)S(1)}, u32[]{:S(2)}, u32[]{:S(2)}) collective-permute-start(bf16[1024,640]{1,0:T(8,128)(2,1)S(1)} %slice.299), channel_id=1, source_target_pairs={{0,1},{1,0},{2,3},{3,2},{4,5},{5,4},{6,7},{7,6},{8,9},{9,8},{10,11... | collective-permute-start | bytes 3932168 | tf_op jit(solution)/shard_map/ppermute | solution.py:68
  555.7 36.0 %collective-permute-start.40 = (bf16[1024,640]{1,0:T(8,128)(2,1)S(1)}, bf16[1024,640]{1,0:T(8,128)(2,1)S(1)}, u32[]{:S(2)}, u32[]{:S(2)}) collective-permute-start(bf16[1024,640]{1,0:T(8,128)(2,1)S(1)} %bitcast.419), channel_id=1, source_target_pairs={{0,1},{1,0},{2,3},{3,2},{4,5},{5,4},{6,7},{7,6},{8,9},{9,8},{10,11... | collective-permute-start | bytes 3932168 | tf_op jit(solution)/shard_map/ppermute | solution.py:68
  558.7 8.9 %collective-permute-start.31 = (bf16[2,2,2,32,640]{4,3,0,1,2:T(8,128)(2,1)S(1)}, bf16[2,2,2,32,640]{4,3,0,1,2:T(8,128)(2,1)S(1)}, u32[]{:S(2)}, u32[]{:S(2)}) collective-permute-start(bf16[2,2,2,32,640]{4,3,0,1,2:T(8,128)(2,1)S(1)} %dynamic-slice_bitcast_fusion.1), channel_id=1, source_target_pairs={{0,8},{1,9},{2,10},{3,11},{4,12},{5,13},{6,14},{7,15},{8,0},{9,1},... | collective-permute-start | bytes 983048 | tf_op jit(solution)/shard_map/ppermute | solution.py:68
  561.7 37.5 %collective-permute-start.45 = (bf16[1024,640]{1,0:T(8,128)(2,1)S(1)}, bf16[1024,640]{1,0:T(8,128)(2,1)S(1)}, u32[]{:S(2)}, u32[]{:S(2)}) collective-permute-start(bf16[1024,640]{1,0:T(8,128)(2,1)S(1)} %bitcast.420), channel_id=1, source_target_pairs={{0,1},{1,0},{2,3},{3,2},{4,5},{5,4},{6,7},{7,6},{8,9},{9,8},{10,11... | collective-permute-start | bytes 3932168 | tf_op jit(solution)/shard_map/ppermute | solution.py:68
  573.9 10.1 %collective-permute-start.26 = (bf16[2,2,2,48,640]{4,3,0,1,2:T(8,128)(2,1)S(1)}, bf16[2,2,2,48,640]{4,3,0,1,2:T(8,128)(2,1)S(1)}, u32[]{:S(2)}, u32[]{:S(2)}) collective-permute-start(bf16[2,2,2,48,640]{4,3,0,1,2:T(8,128)(2,1)S(1)} %dynamic-slice_bitcast_fusion), channel_id=1, source_target_pairs={{0,2},{1,3},{2,0},{3,1},{4,6},{5,7},{6,4},{7,5},{8,10},{9,11},{10,... | collective-permute-start | bytes 1474568 | tf_op jit(solution)/shard_map/ppermute | solution.py:68
  584.2 6.3 collective-permute-start.27
  586.5 19.2 %collective-permute-start.36 = (bf16[512,640]{1,0:T(8,128)(2,1)S(1)}, bf16[512,640]{1,0:T(8,128)(2,1)S(1)}, u32[]{:S(2)}, u32[]{:S(2)}) collective-permute-start(bf16[512,640]{1,0:T(8,128)(2,1)S(1)} %slice.301), channel_id=1, source_target_pairs={{0,2},{1,3},{2,0},{3,1},{4,6},{5,7},{6,4},{7,5},{8,10},{9,11},{10,... | collective-permute-start | bytes 1966088 | tf_op jit(solution)/shard_map/ppermute | solution.py:68
  590.5 6.3 collective-permute-start.28
  592.0 15.4 %collective-permute-start.41 = (bf16[512,640]{1,0:T(8,128)(2,1)S(1)}, bf16[512,640]{1,0:T(8,128)(2,1)S(1)}, u32[]{:S(2)}, u32[]{:S(2)}) collective-permute-start(bf16[512,640]{1,0:T(8,128)(2,1)S(1)} %slice.311), channel_id=1, source_target_pairs={{0,8},{1,9},{2,10},{3,11},{4,12},{5,13},{6,14},{7,15},{8,0},{9,1},... | collective-permute-start | bytes 1966088 | tf_op jit(solution)/shard_map/ppermute | solution.py:68
  596.9 7.5 %collective-permute-start.29 = (bf16[48,640]{1,0:T(8,128)(2,1)S(1)}, bf16[48,640]{1,0:T(8,128)(2,1)S(1)}, u32[]{:S(2)}, u32[]{:S(2)}) collective-permute-start(bf16[48,640]{1,0:T(8,128)(2,1)S(1)} %dynamic-slice_bitcast_fusion.6), channel_id=1, source_target_pairs={{0,16},{1,17},{2,18},{3,19},{4,20},{5,21},{6,22},{7,23},{8,24},{9,... | collective-permute-start | bytes 184328 | tf_op jit(solution)/shard_map/ppermute | solution.py:68
  599.6 13.2 %collective-permute-start.46 = (bf16[512,640]{1,0:T(8,128)(2,1)S(1)}, bf16[512,640]{1,0:T(8,128)(2,1)S(1)}, u32[]{:S(2)}, u32[]{:S(2)}) collective-permute-start(bf16[512,640]{1,0:T(8,128)(2,1)S(1)} %slice.321), channel_id=1, source_target_pairs={{0,4},{1,5},{2,6},{3,7},{4,0},{5,1},{6,2},{7,3},{8,12},{9,13},{10,... | collective-permute-start | bytes 1966088 | tf_op jit(solution)/shard_map/ppermute | solution.py:68
  605.9 11.2 %collective-permute-start.37 = (bf16[256,640]{1,0:T(8,128)(2,1)S(1)}, bf16[256,640]{1,0:T(8,128)(2,1)S(1)}, u32[]{:S(2)}, u32[]{:S(2)}) collective-permute-start(bf16[256,640]{1,0:T(8,128)(2,1)S(1)} %slice.303), channel_id=1, source_target_pairs={{0,4},{1,5},{2,6},{3,7},{4,0},{5,1},{6,2},{7,3},{8,12},{9,13},{10,... | collective-permute-start | bytes 983048 | tf_op jit(solution)/shard_map/ppermute | solution.py:68
  607.6 13.0 %collective-permute-start.42 = (bf16[256,640]{1,0:T(8,128)(2,1)S(1)}, bf16[256,640]{1,0:T(8,128)(2,1)S(1)}, u32[]{:S(2)}, u32[]{:S(2)}) collective-permute-start(bf16[256,640]{1,0:T(8,128)(2,1)S(1)} %slice.313), channel_id=1, source_target_pairs={{0,2},{1,3},{2,0},{3,1},{4,6},{5,7},{6,4},{7,5},{8,10},{9,11},{10,... | collective-permute-start | bytes 983048 | tf_op jit(solution)/shard_map/ppermute | solution.py:68
  613.0 9.3 %collective-permute-start.47 = (bf16[256,640]{1,0:T(8,128)(2,1)S(1)}, bf16[256,640]{1,0:T(8,128)(2,1)S(1)}, u32[]{:S(2)}, u32[]{:S(2)}) collective-permute-start(bf16[256,640]{1,0:T(8,128)(2,1)S(1)} %slice.323), channel_id=1, source_target_pairs={{0,8},{1,9},{2,10},{3,11},{4,12},{5,13},{6,14},{7,15},{8,0},{9,1},... | collective-permute-start | bytes 983048 | tf_op jit(solution)/shard_map/ppermute | solution.py:68
  617.2 8.3 %collective-permute-start.38 = (bf16[128,640]{1,0:T(8,128)(2,1)S(1)}, bf16[128,640]{1,0:T(8,128)(2,1)S(1)}, u32[]{:S(2)}, u32[]{:S(2)}) collective-permute-start(bf16[128,640]{1,0:T(8,128)(2,1)S(1)} %slice.305), channel_id=1, source_target_pairs={{0,8},{1,9},{2,10},{3,11},{4,12},{5,13},{6,14},{7,15},{8,0},{9,1},... | collective-permute-start | bytes 491528 | tf_op jit(solution)/shard_map/ppermute | solution.py:68
  620.7 6.0 collective-permute-start.43
  622.4 6.3 collective-permute-start.48
  626.8 6.9 %collective-permute-start.44 = (bf16[64,640]{1,0:T(8,128)(2,1)S(1)}, bf16[64,640]{1,0:T(8,128)(2,1)S(1)}, u32[]{:S(2)}, u32[]{:S(2)}) collective-permute-start(bf16[64,640]{1,0:T(8,128)(2,1)S(1)} %slice.317), channel_id=1, source_target_pairs={{0,16},{1,17},{2,18},{3,19},{4,20},{5,21},{6,22},{7,23},{8,24},{9,... | collective-permute-start | bytes 245768 | tf_op jit(solution)/shard_map/ppermute | solution.py:68
  628.8 6.6 %collective-permute-start.49 = (bf16[64,640]{1,0:T(8,128)(2,1)S(1)}, bf16[64,640]{1,0:T(8,128)(2,1)S(1)}, u32[]{:S(2)}, u32[]{:S(2)}) collective-permute-start(bf16[64,640]{1,0:T(8,128)(2,1)S(1)} %slice.327), channel_id=1, source_target_pairs={{0,16},{1,17},{2,18},{3,19},{4,20},{5,21},{6,22},{7,23},{8,24},{9,... | collective-permute-start | bytes 245768 | tf_op jit(solution)/shard_map/ppermute | solution.py:68
  (137 other events, 1442.9 us)
